TPU v7x, 32 devices: a whole 2x2x4 slice. The times are simulated.
32 devices in a mesh: expert: 4 (over z), mp: 4 (over y, core), replica: 2 (over x).
Axes of the slice: x: 2, y: 2, z: 4, core: 2. Of those that a mesh axis runs over, the one named last changes fastest.
Arguments:
- grad_out: bfloat16 [2, 512, 2080], P('replica', 'expert')
- route: int32 [2, 512, 1], P('replica', 'expert'), may hold values from 0 to 3; in each aligned block of 128 rows (0 to 127, 128 to 255, ..., all dimensions but the last counted through in order) at most 48 rows name the same one
- hidden_act: bfloat16 [2, 4, 192, 6144], P('replica', 'expert', None, 'mp'), as said below
- out_weight: bfloat16 [4, 6144, 2080], P('expert', 'mp'), may hold values from -0.078125 to 0.078125
- row_state: float32 [4, 6144], P('expert', ('mp', 'replica')), may hold values from 0.01 to 0.3
- col_state: float32 [4, 2080], P('expert'), as said below
Outputs:
- hidden_grad: bfloat16 [2, 4, 192, 6144], P('replica', 'expert', None, 'mp')
- update: float32 [4, 6144, 2080], P('expert', ('mp', 'replica'))
- row_new: float32 [4, 6144], P('expert', ('mp', 'replica'))
- col_new: float32 [4, 2080], P('expert')
Inputs may be any that keep to these rules, and one draw needn't show every extreme that they name: `route`: in each aligned block of 128 tokens (the tokens of one index of expert) no expert is named more than 48 times, a bound that some block reaches. `hidden_act`: non-negative. `col_state`: positive.
All inputs are finite; a program needn't handle non-finite values.
Results may differ from a plain program's by a relative error of at most 0.001.
Values may be sent and summed in bfloat16 or wider, within the bound.
A program may use at most 128 MiB of HBM per device.

v0:
```python
import jax
import jax.numpy as jnp
from jax import lax
from jax.sharding import PartitionSpec as P

FF = 6144
EXP_DEV = 1


decay_rate = 0.8
clip_limit = 1.0
tiny_square = 1e-30


def on_device(grad_out, route, hidden_act, out_weight, row_state, col_state):
    n_expert = lax.axis_size("expert")
    tok_count = grad_out.shape[1]
    width = grad_out.shape[2]
    experts = EXP_DEV * n_expert
    capacity = 3 * tok_count // (2 * experts)
    tokens = grad_out[0]
    expert_ids = route[0, :, 0]
    onehot = (expert_ids[:, None] == jnp.arange(experts, dtype=jnp.int32)[None, :]).astype(
        jnp.float32
    )
    row_iota = lax.broadcasted_iota(jnp.int32, (tok_count, tok_count), 0)
    col_iota = lax.broadcasted_iota(jnp.int32, (tok_count, tok_count), 1)
    earlier = (row_iota > col_iota).astype(jnp.float32)
    position = jnp.sum(
        jnp.dot(earlier, onehot, preferred_element_type=jnp.float32) * onehot, axis=1
    ).astype(jnp.int32)
    slot_index = expert_ids * capacity + position
    dispatch = (
        slot_index[None, :] == jnp.arange(experts * capacity, dtype=jnp.int32)[:, None]
    ).astype(jnp.bfloat16)
    outgoing = jnp.dot(dispatch, tokens, preferred_element_type=jnp.float32).astype(jnp.bfloat16)
    outgoing = outgoing.reshape(n_expert, EXP_DEV * capacity, width)
    arrived = lax.all_to_all(outgoing, "expert", split_axis=0, concat_axis=0, tiled=True)
    arrived = arrived.reshape(n_expert, EXP_DEV, capacity, width).transpose(1, 0, 2, 3)
    arrived = arrived.reshape(EXP_DEV, n_expert * capacity, width)
    hidden = hidden_act[0]
    hidden_grad = jnp.einsum(
        "esd,efd->esf", arrived, out_weight, preferred_element_type=jnp.float32
    )
    hidden_grad = hidden_grad.astype(jnp.bfloat16)[None]
    parts = lax.all_to_all(hidden, "replica", split_axis=2, concat_axis=1, tiled=True)
    grad = jnp.einsum(
        "esf,esd->efd",
        parts,
        lax.all_gather(arrived, "replica", axis=1, tiled=True),
        preferred_element_type=jnp.float32,
    )
    squares = grad * grad + tiny_square
    row_new = decay_rate * row_state + (1.0 - decay_rate) * jnp.mean(squares, axis=2)
    col_part = jnp.sum(squares, axis=1)
    row_part = jnp.sum(row_new, axis=1)
    weighted = jnp.sum(grad * grad / row_new[:, :, None], axis=1)
    col_total, weighted_total, row_total = lax.psum(
        (col_part, weighted, row_part), ("mp", "replica")
    )
    col_new = decay_rate * col_state + (1.0 - decay_rate) * col_total / FF
    row_mean = row_total / FF
    raw_step = grad / jnp.sqrt(row_new[:, :, None] * col_new[:, None, :] / row_mean[:, None, None])
    update_sq = row_mean * jnp.sum(weighted_total / col_new, axis=1)
    update_rms = jnp.sqrt(update_sq / (FF * width))
    update = raw_step / jnp.maximum(1.0, update_rms / clip_limit)[:, None, None]
    return (hidden_grad, update, row_new, col_new)


def solution(mesh):
    in_specs = (
        P("replica", "expert", None),
        P("replica", "expert", None),
        P("replica", "expert", None, "mp"),
        P("expert", "mp", None),
        P("expert", ("mp", "replica")),
        P("expert", None),
    )
    out_specs = (
        P("replica", "expert", None, "mp"),
        P("expert", ("mp", "replica"), None),
        P("expert", ("mp", "replica")),
        P("expert", None),
    )
    return jax.shard_map(
        on_device, mesh=mesh, in_specs=in_specs, out_specs=out_specs, check_vma=False
    )
```

profile of v0, /device:TPU:0, one launch (start us, length us, event | category | flops | bytes accessed | tf_op | source)
XLA Modules:
  0.0 123.5 jit_solution(1001607644345151885)
XLA Ops:
  7.2 0.0 copy-start
  7.2 0.0 all-gather.2.cloned.1.call-start
  7.2 0.9 fusion.15
  8.1 0.7 convert_add_fusion
  8.8 0.4 convolution_convert_fusion
  9.2 27.4 %all_to_all.20 = bf16[4,48,2080]{2,1,0:T(8,128)(2,1)} all-to-all(bf16[4,48,2080]{2,1,0:T(8,128)(2,1)S(1)} %bitcast.54), channel_id=1, replica_groups=mesh['expert'=4,'mp'=4,'replica'=2] {'expert'}, dimensions={0} | all-to-all | bytes 1597440 | tf_op jit(solution)/shard_map/all_to_all | solution.py:38
  36.6 0.0 all-gather.2.cloned.1.call-update
  36.6 3.5 %copy.14 = bf16[1,192,1536]{1,0,2:T(2,128)(2,1)S(1)} copy(bf16[1,192,1536]{2,1,0:T(8,128)(2,1)} %bitcast.57) | data formatting | bytes 1179648 | tf_op jit(solution)/shard_map/squeeze | solution.py:41
  40.1 0.5 broadcast.35
  40.7 9.8 %reduce.12 = bf16[1536,192]{1,0:T(8,128)(2,1)} reduce(bf16[1536,1,192]{2,1,0:T(2,128)(2,1)S(1)} %bitcast.50, bf16[]{:T(256)} %broadcast.35), dimensions={1}, to_apply=%bitcast.44.reduce_sub_computation | reduce | bytes 1179650
  50.4 1.9 %reshape.81 = bf16[2,2,73728]{2,1,0:T(2,128)(2,1)S(1)} reshape(bf16[1536,192]{1,0:T(8,128)(2,1)} %reduce.12) | data formatting | bytes 1179648
  52.4 17.9 %all_to_all.21 = bf16[2,2,73728]{2,1,0:T(2,128)(2,1)S(1)} all-to-all(bf16[2,2,73728]{2,1,0:T(2,128)(2,1)S(1)} %reshape.81), channel_id=1, replica_groups=mesh['expert'=4,'mp'=4,'replica'=2] {'replica'}, dimensions={0} | all-to-all | bytes 1179648 | tf_op jit(solution)/shard_map/all_to_all | solution.py:46
  70.2 1.1 reshape.82
  71.3 0.9 copy.15
  72.3 0.1 all_to_all.16
  72.4 0.1 copy.16
  72.5 5.2 %fusion.10 = bf16[1,1,192,1536]{3,2,1,0:T(8,128)(2,1)} fusion(bf16[192,2080]{1,0:T(8,128)(2,1)S(1)} %bitcast.53, bf16[1,1536,2080]{1,2,0:T(8,128)(2,1)} %param.9), kind=kOutput, calls=%fused_computation.12 | convolution fusion | flops 1227128832 | bytes 7778304 | tf_op jit(solution)/shard_map/esd,efd->esf/dot_general | solution.py:42
  77.7 3.4 %fusion.6 = (f32[768]{0:T(1024)S(1)}, f32[2080,768]{1,0:T(8,128)S(1)}) fusion(bf16[384,768]{1,0:T(8,128)(2,1)S(1)} %bitcast.56, bf16[1,384,2080]{2,1,0:T(8,128)(2,1)} %all-gather.2.cloned.1.call-done), kind=kOutput, calls=%fused_computation.9 | convolution fusion | flops 1231625472 | bytes 8580096 | tf_op jit(solution)/shard_map/esf,esd->efd/dot_general | solution.py:47
  81.1 1.7 %fusion.20 = (f32[768]{0:T(1024)S(1)}, f32[]{:T(128)}, f32[1,768]{1,0:T(1,128)}) fusion(f32[768]{0:T(1024)S(1)} %broadcast_multiply_fusion, f32[1,768]{1,0:T(1,128)S(1)} %copy-done.4), kind=kLoop, calls=%fused_computation.29 | loop fusion | flops 2303 | bytes 12292 | tf_op jit(solution)/shard_map/add | solution.py:54
  82.7 1.1 copy-done.1
  83.8 1.2 fusion.5
  85.0 23.9 %all-reduce = (f32[1]{0:T(128)}, f32[1,2080]{1,0:T(1,128)S(1)}, f32[1,2080]{1,0:T(1,128)S(1)}) all-reduce(f32[1]{0:T(128)} %bitcast.12, f32[1,2080]{1,0:T(1,128)S(1)} %reduce_sum.65, f32[1,2080]{1,0:T(1,128)S(1)} %reduce_sum.69), channel_id=1, replica_groups=mesh['expert'=4,'mp'=4,'replica'=2] {'mp','replica'}, use_global_device_ids=true, to_apply=%region_5.0 | all-reduce | flops 4161 | bytes 33288 | tf_op jit(solution)/shard_map/psum | solution.py:58
  109.5 1.2 fusion.19
  111.3 5.3 %fusion.1 = f32[1,768,2080]{1,2,0:T(8,128)} fusion(f32[2080,768]{1,0:T(8,128)} %copy-done.1, f32[]{:T(128)} %bitcast.15, f32[]{:T(128)} %bitcast.13, f32[2080]{0:T(1024)S(1)} %get-tuple-element.6, f32[768]{0:T(1024)S(1)} %get-tuple-element.8), kind=kLoop, calls=%fused_computation.3 | loop fusion | flops 6389760 | bytes 12790920 | tf_op jit(solution)/shard_map/div | solution.py:66
  (12 shorter events, 0.0 us)
Async XLA Ops:
  7.2 1.6 %copy-start = (bf16[1,128,2080]{1,2,0:T(8,128)(2,1)S(1)}, bf16[1,128,2080]{1,2,0:T(8,128)(2,1)}, u32[]{:S(2)}) copy-start(bf16[1,128,2080]{1,2,0:T(8,128)(2,1)} %param.6) | copy-start | bytes 1597444
  7.2 70.5 %all-gather.2.cloned.1.call-start = ((), (), s32[]{:S(2)}) async-start(), calls=%async_computation.2 | async-start | bytes 2506752 | tf_op jit(solution)/shard_map/all_gather | solution.py:50
  36.6 35.9 %copy-start.2 = (bf16[4,48,2080]{2,1,0:T(8,128)(2,1)S(1)}, bf16[4,48,2080]{2,1,0:T(8,128)(2,1)}, u32[]{:S(2)}) copy-start(bf16[4,48,2080]{2,1,0:T(8,128)(2,1)} %all_to_all.20) | copy-start | bytes 2396164
  77.7 3.4 %copy-start.4 = (f32[1,768]{1,0:T(1,128)S(1)}, f32[1,768]{1,0:T(1,128)}, u32[]{:S(2)}) copy-start(f32[1,768]{1,0:T(1,128)} %param.10) | copy-start | bytes 9220
  77.7 31.8 %copy-start.3 = (f32[1,2080]{1,0:T(1,128)S(1)}, f32[1,2080]{1,0:T(1,128)}, u32[]{:S(2)}) copy-start(f32[1,2080]{1,0:T(1,128)} %param.11) | copy-start | bytes 24964
  81.0 2.7 %copy-start.1 = (f32[2080,768]{1,0:T(8,128)}, f32[2080,768]{1,0:T(8,128)S(1)}, u32[]{:S(2)}) copy-start(f32[2080,768]{1,0:T(8,128)S(1)} %get-tuple-element.16) | copy-start | bytes 19169284
Sparse Core Ops, SparseCore 0:
  36.7 33.6 all-gather.1
where the time goes:
time: 124 us; the launch traced here: 123 us
  blocking collectives  69.1 us (56%)
  other arithmetic  19.8 us (16%)
  between operations  15.4 us (12%)
  matrix products  9.79 us (8%)
  local copies, waits for them, and re-layouts  9.27 us (7%)
    all_to_all x1, blocking collectives, on_device(): lax.all_to_all(outgoing, 'expert', split_axis=0, concat_axis=0, tiled=True)  27.4 us
    psum x1, blocking collectives, on_device(): lax.psum((col_part, weighted, row_part), ('mp', 'replica'))  23.9 us
    all_to_all x1, blocking collectives, on_device(): lax.all_to_all(hidden, 'replica', split_axis=2, concat_axis=1, tiled=True)  17.9 us
    unnamed x1, other arithmetic  9.77 us
    div x1, other arithmetic, on_device(): update = raw_step / jnp.maximum(1.0, update_rms / clip_limit)[:, None, None]  5.33 us
    dot_general x1, matrix products, on_device(): jnp.einsum('esd,efd->esf', arrived, out_weight, preferred_element_type=jn...  5.17 us
    unnamed x13, local copies, waits for them, and re-layouts  4.6 us
    squeeze x1, local copies, waits for them, and re-layouts, on_device(): hidden = hidden_act[0]  3.53 us
  transfers between devices with their start and end apart: 1, of which 0 were waited for; matrix products, arithmetic and copies ran while one was open for 19% of the time, Pallas kernels for 0%

commit v1 on v0

--- a/solution.py
+++ b/solution.py
@@ -1,6 +1,10 @@
+import functools
+
 import jax
 import jax.numpy as jnp
 from jax import lax
+from jax.experimental import pallas as pl
+from jax.experimental.pallas import tpu as pltpu
 from jax.sharding import PartitionSpec as P
 
 FF = 6144
@@ -67,6 +71,287 @@
     return (hidden_grad, update, row_new, col_new)
 
 
+MESH = pl.DeviceIdType.MESH
+CH = 512
+REM = 128
+
+
+def exchange_kernel(
+    n, cap, tok_ref, ids_ref, hid_ref, w_hbm, row_ref, col_ref,
+    hg_ref, rownew_ref, colnew_ref, cfac_ref, rfac_ref, ht_hbm, rec_hbm,
+    outb, zb, parts, hs, ht, w, st, rowcol, w_sem, loc_sem, send_sem, recv_sem,
+):
+    e = lax.axis_index("expert")
+    m = lax.axis_index("mp")
+    r = lax.axis_index("replica")
+    width = tok_ref.shape[1]
+    slots = n * cap
+    half = hs.shape[1]
+    rem = width - 4 * CH
+    f32 = jnp.float32
+
+    w_copy = pltpu.make_async_copy(w_hbm, w, w_sem)
+    w_copy.start()
+
+    def across(d):
+        m2 = m + (1 - 2 * (m % 2)) * (d % 2)
+        m2 = m2 + (2 - 4 * (m // 2)) * ((d // 2) % 2)
+        r2 = r + (1 - 2 * r) * (d // 4)
+        return (e, m2, r2)
+
+    def along(k):
+        return (lax.rem(e + k, n), m, r)
+
+    barrier = pltpu.get_barrier_semaphore()
+    for d in range(1, 8):
+        pl.semaphore_signal(barrier, inc=1, device_id=across(d), device_id_type=MESH)
+    for k in range(1, n):
+        pl.semaphore_signal(barrier, inc=1, device_id=along(k), device_id_type=MESH)
+
+    tc = tok_ref.shape[0]
+    ids = jnp.broadcast_to(ids_ref[...].astype(f32), (tc, tc))
+    ids_t = ids.T
+    p_i = lax.broadcasted_iota(jnp.int32, (tc, tc), 0)
+    q_i = lax.broadcasted_iota(jnp.int32, (tc, tc), 1)
+    before = jnp.where((p_i < q_i) & (ids == ids_t), 1.0, 0.0)
+    slot = ids_t[0:1, :] * cap + jnp.sum(before, axis=0, keepdims=True)
+    want = lax.broadcasted_iota(jnp.int32, (slots, tc), 0).astype(f32)
+    dispatch = jnp.where(want == slot, 1.0, 0.0).astype(jnp.bfloat16)
+    mine = tok_ref[:, pl.ds(pl.multiple_of(m * CH, CH), CH)]
+    outb[:, 0:CH] = jnp.dot(dispatch, mine, preferred_element_type=f32).astype(jnp.bfloat16)
+    outb[:, CH:] = jnp.zeros((slots, REM), jnp.bfloat16)
+    outb[:, CH:CH + rem] = jnp.dot(
+        dispatch, tok_ref[:, 4 * CH:], preferred_element_type=f32
+    ).astype(jnp.bfloat16)
+    pl.semaphore_wait(barrier, 7 + n - 1)
+
+    started = []
+
+    def send(src, dst, to):
+        i = len(started)
+        c = pltpu.make_async_remote_copy(
+            src_ref=src, dst_ref=dst, send_sem=send_sem.at[i], recv_sem=recv_sem.at[i],
+            device_id=to, device_id_type=MESH,
+        )
+        c.start()
+        started.append(c)
+        return c
+
+    def rows_of(k, base=0):
+        return pl.ds(pl.multiple_of(base + lax.rem(e - k + n, n) * cap, 16), cap)
+
+    own = rows_of(0)
+    zc = [None]
+    for k in range(1, n):
+        there = pl.ds(pl.multiple_of(lax.rem(e + k, n) * cap, 16), cap)
+        zc.append(send(outb.at[there, :], zb.at[own, :], along(k)))
+    zb[own, :] = outb[own, :]
+    other_half = pl.ds(pl.multiple_of((1 - r) * half, 128), half)
+    own_half = pl.ds(pl.multiple_of(r * half, 128), half)
+    xc, hc, yo, co = [], [], [], []
+    for k in range(n):
+        if k:
+            zc[k].wait_recv()
+        a, b = rows_of(k), rows_of(k, slots)
+        xc.append(send(zb.at[a, :], zb.at[b, :], across(4)))
+        yo.append(send(zb.at[a, 0:CH], parts.at[m, a, :], across(2)))
+        co.append(send(zb.at[a, 0:CH], parts.at[m, a, :], across(1)))
+        piece = pl.ds(k * cap, cap)
+        there = pl.ds(slots + k * cap, cap)
+        hc.append(send(hid_ref.at[piece, other_half], hs.at[there, :], across(4)))
+    m_y = across(2)[1]
+    parts[m, 0:slots, :] = zb[0:slots, 0:CH]
+    hs[0:slots, :] = hid_ref[:, own_half]
+    fo, yx, cx, fx = [], [], [], []
+    for k in range(n):
+        yo[k].wait_recv()
+        a = rows_of(k)
+        fo.append(send(parts.at[m_y, a, :], parts.at[m_y, a, :], across(1)))
+    for k in range(n):
+        xc[k].wait_recv()
+        b = rows_of(k, slots)
+        yx.append(send(zb.at[b, 0:CH], parts.at[m, b, :], across(2)))
+        cx.append(send(zb.at[b, 0:CH], parts.at[m, b, :], across(1)))
+    for k in range(n):
+        co[k].wait_recv()
+        fo[k].wait_recv()
+    w_copy.wait()
+
+    nt = (((1,), (1,)), ((), ()))
+
+    def hidden_tile(t):
+        f = pl.ds(pl.multiple_of(t * 256, 256), 256)
+        acc = lax.dot_general(
+            zb[0:slots, CH:CH + rem], w[f, 4 * CH:], nt, preferred_element_type=f32
+        )
+        for c in range(4):
+            acc += lax.dot_general(
+                parts[c, 0:slots, :], w[f, c * CH:(c + 1) * CH], nt, preferred_element_type=f32
+            )
+        hg_ref[:, f] = acc.astype(jnp.bfloat16)
+
+    tiles = hg_ref.shape[1] // 256
+    for k in range(n):
+        lo, hi = tiles * k // n, tiles * (k + 1) // n
+
+        def some(t, carry):
+            hidden_tile(t)
+            return carry
+
+        lax.fori_loop(lo, hi, some, 0)
+        yx[k].wait_recv()
+        b = rows_of(k, slots)
+        fx.append(send(parts.at[m_y, b, :], parts.at[m_y, b, :], across(1)))
+    parts[m, slots:, :] = zb[slots:, 0:CH]
+    for k in range(n):
+        hc[k].wait_recv()
+        cx[k].wait_recv()
+        fx[k].wait_recv()
+
+    local = []
+    for c in range(4):
+        local.append(pltpu.make_async_copy(
+            parts.at[c], rec_hbm.at[:, pl.ds(c * CH, CH)], loc_sem.at[c]))
+    local.append(pltpu.make_async_copy(
+        zb.at[:, pl.ds(CH, REM)], rec_hbm.at[:, pl.ds(4 * CH, REM)], loc_sem.at[4]))
+    for c in local:
+        c.start()
+
+    rowcol[...] = jnp.broadcast_to(row_ref[...], (128, half)).T
+    blk = 128
+
+    def block(t, carry):
+        total, cols, weights = carry
+        i = pl.ds(pl.multiple_of(t * blk, blk), blk)
+        h = hs[:, i].T
+        ht[i, :] = h
+        gg = []
+        for c in range(5):
+            rhs = parts[c] if c < 4 else zb[:, CH:CH + REM]
+            g = jnp.dot(h, rhs, preferred_element_type=f32)
+            gg.append(g * g)
+        rs = sum(jnp.sum(x, axis=1, keepdims=True) for x in gg)
+        mean = rs / width + tiny_square
+        new = decay_rate * rowcol[i, 0:1] + (1.0 - decay_rate) * mean
+        rfac_ref[i, :] = lax.rsqrt(new)
+        rowcol[i, :] = jnp.broadcast_to(new, (blk, 128))
+        inv = 1.0 / new
+        total = total + jnp.sum(new, axis=0, keepdims=True)
+        cols = tuple(
+            a + jnp.sum(x, axis=0, keepdims=True) for a, x in zip(cols, gg))
+        weights = tuple(
+            a + jnp.sum(x * inv, axis=0, keepdims=True) for a, x in zip(weights, gg))
+        return total, cols, weights
+
+    zero = tuple(jnp.zeros((1, CH if c < 4 else REM), f32) for c in range(5))
+    total, cols, weights = lax.fori_loop(
+        0, half // blk, block, (jnp.zeros((1, 1), f32), zero, zero))
+    me = m * 2 + r
+    cols = [x + half * tiny_square for x in cols]
+    for j in range(17):
+        c, o = j // 4, (j % 4) * 128
+        st[me, j:j + 1, :] = cols[c][:, o:o + 128]
+        st[me, 17 + j:18 + j, :] = weights[c][:, o:o + 128]
+    st[me, 34:35, :] = jnp.broadcast_to(total, (1, 128))
+    st[me, 35:40, :] = jnp.zeros((5, 128), f32)
+    sc = [send(st.at[me], st.at[me], across(d)) for d in range(1, 8)]
+    ht_copy = pltpu.make_async_copy(ht, ht_hbm, loc_sem.at[5])
+    ht_copy.start()
+    rownew_ref[...] = rowcol[...].T[0:1, :]
+    for c in sc:
+        c.wait_recv()
+    tot = st[0]
+    for j in range(1, 8):
+        tot = tot + st[j]
+
+    def flat(base):
+        x = jnp.concatenate([tot[base + j:base + j + 1, :] for j in range(17)], axis=1)
+        return x[:, 0:width]
+
+    col_new = decay_rate * col_ref[...] + (1.0 - decay_rate) * (flat(0) / FF)
+    row_mean = tot[34:35, 0:1] / FF
+    colnew_ref[...] = col_new
+    ratio = jnp.sum(flat(17) / col_new, axis=1, keepdims=True)
+    rms = jnp.sqrt(row_mean * ratio / (FF * width))
+    scale = jnp.sqrt(row_mean) / jnp.maximum(1.0, rms / clip_limit)
+    cfac_ref[...] = lax.rsqrt(col_new) * scale
+    for c in started:
+        c.wait_send()
+    for c in local:
+        c.wait()
+    ht_copy.wait()
+
+
+def update_kernel(ht_ref, rec_ref, rfac_ref, cfac_ref, out_ref):
+    width = out_ref.shape[1]
+    h = ht_ref[...]
+    rf = rfac_ref[...]
+    for c in range(5):
+        lo, hi = c * CH, min(width, (c + 1) * CH)
+        g = jnp.dot(h, rec_ref[:, lo:hi], preferred_element_type=jnp.float32)
+        out_ref[:, lo:hi] = (g * rf) * cfac_ref[:, lo:hi]
+
+
+def fused(grad_out, route, hidden_act, out_weight, row_state, col_state):
+    n = lax.axis_size("expert")
+    tok_count, width = grad_out.shape[1:]
+    cap = 3 * tok_count // (2 * n)
+    slots = n * cap
+    ff = hidden_act.shape[3]
+    half = ff // 2
+    bf16, f32 = jnp.bfloat16, jnp.float32
+    vmem = pl.BlockSpec(memory_space=pltpu.VMEM)
+    hbm = pl.BlockSpec(memory_space=pl.ANY)
+    wide = 4 * CH + REM
+    copies = 9 * n + n - 1 + 7
+    hg, row_new, col_new, cfac, rfac, ht, rec = pl.pallas_call(
+        functools.partial(exchange_kernel, n, cap),
+        out_shape=[
+            jax.ShapeDtypeStruct((slots, ff), bf16),
+            jax.ShapeDtypeStruct((1, half), f32),
+            jax.ShapeDtypeStruct((1, width), f32),
+            jax.ShapeDtypeStruct((1, width), f32),
+            jax.ShapeDtypeStruct((half, 1), f32),
+            jax.ShapeDtypeStruct((half, 2 * slots), bf16),
+            jax.ShapeDtypeStruct((2 * slots, wide), bf16),
+        ],
+        in_specs=[vmem, vmem, vmem, hbm, vmem, vmem],
+        out_specs=[vmem] * 5 + [hbm] * 2,
+        scratch_shapes=[
+            pltpu.VMEM((slots, CH + REM), bf16),
+            pltpu.VMEM((2 * slots, CH + REM), bf16),
+            pltpu.VMEM((4, 2 * slots, CH), bf16),
+            pltpu.VMEM((2 * slots, half), bf16),
+            pltpu.VMEM((half, 2 * slots), bf16),
+            pltpu.VMEM((ff, width), bf16),
+            pltpu.VMEM((8, 40, 128), f32),
+            pltpu.VMEM((half, 128), f32),
+            pltpu.SemaphoreType.DMA,
+            pltpu.SemaphoreType.DMA((6,)),
+            pltpu.SemaphoreType.DMA((copies,)),
+            pltpu.SemaphoreType.DMA((copies,)),
+        ],
+        compiler_params=pltpu.CompilerParams(
+            collective_id=0, has_side_effects=True, vmem_limit_bytes=40 * 1024 * 1024
+        ),
+    )(grad_out[0], route[0], hidden_act[0, 0], out_weight[0], row_state, col_state)
+    blk = 128
+    update = pl.pallas_call(
+        update_kernel,
+        grid=(half // blk,),
+        out_shape=jax.ShapeDtypeStruct((half, width), f32),
+        in_specs=[
+            pl.BlockSpec((blk, 2 * slots), lambda i: (i, 0)),
+            pl.BlockSpec((2 * slots, wide), lambda i: (0, 0)),
+            pl.BlockSpec((blk, 1), lambda i: (i, 0)),
+            pl.BlockSpec((1, width), lambda i: (0, 0)),
+        ],
+        out_specs=pl.BlockSpec((blk, width), lambda i: (i, 0)),
+        compiler_params=pltpu.CompilerParams(vmem_limit_bytes=32 * 1024 * 1024),
+    )(ht, rec, rfac, cfac)
+    return hg[None, None], update[None], row_new, col_new
+
+
 def solution(mesh):
     in_specs = (
         P("replica", "expert", None),
@@ -82,6 +367,9 @@
         P("expert", ("mp", "replica")),
         P("expert", None),
     )
+    n = mesh.shape["expert"]
+    whole_tiles = 48 * 4 // n % 16 == 0
+    body = fused if whole_tiles and mesh.shape["mp"] == 4 and mesh.shape["replica"] == 2 else on_device
     return jax.shard_map(
-        on_device, mesh=mesh, in_specs=in_specs, out_specs=out_specs, check_vma=False
-    )
+        body, mesh=mesh, in_specs=in_specs, out_specs=out_specs, check_vma=False
+    )

time: 124 us -> 64.1 us (0.52)
  blocking collectives: 69.1 us -> 0 us
  Pallas kernels: 0 us -> 36.6 us
  other arithmetic: 19.8 us -> 0 us
  local copies, waits for them, and re-layouts: 9.27 us -> 26.3 us
  between operations: 15.4 us -> 0.7 us
  matrix products: 9.79 us -> 0 us
    all_to_all x2 -> x0, blocking collectives: 45.3 us -> none  [the longest x1 27.4 us: on_device(): lax.all_to_all(outgoing, 'expert', split_axis=0, concat_axis=0, tiled=True)]
    pallas_call x0 -> x2, Pallas kernels: none -> 36.6 us  [the longest x1 33.6 us: fused(): pl.pallas_call(functools.partial(exchange_kernel, n, cap), out_shape=[jax...]
    psum x1 -> x0, blocking collectives: 23.9 us -> none  [on_device(): lax.psum((col_part, weighted, row_part), ('mp', 'replica'))]
    unnamed x13 -> x16, local copies, waits for them, and re-layouts: 4.6 us -> 25.6 us
    dot_general x4 -> x0, matrix products: 9.79 us -> none  [the longest x1 5.17 us: on_device(): jnp.einsum('esd,efd->esf', arrived, out_weight, preferred_element_type=jn...]
    unnamed x1 -> x0, other arithmetic: 9.77 us -> none
    div x1 -> x0, other arithmetic: 5.33 us -> none  [on_device(): update = raw_step / jnp.maximum(1.0, update_rms / clip_limit)[:, None, None]]
    add x3 -> x0, other arithmetic: 3.55 us -> none  [the longest x1 1.66 us: on_device(): decay_rate * row_state + (1.0 - decay_rate) * jnp.mean(squares, axis=2)]
  transfers between devices with their start and end apart: 1 -> 0, of which waited for: 0 -> 0; matrix products, arithmetic and copies ran while one was open for 19% -> 0% of each run, Pallas kernels for 0% -> 0%
where the time goes in v1:
time: 64.1 us; the launch traced here: 63.6 us
  Pallas kernels  36.6 us (57%)
  local copies, waits for them, and re-layouts  26.3 us (41%)
  between operations  0.7 us (1%)
    pallas_call x1, Pallas kernels, fused(): pl.pallas_call(functools.partial(exchange_kernel, n, cap), out_shape=[jax...  33.6 us
    unnamed x16, local copies, waits for them, and re-layouts  25.6 us
    pallas_call x1, Pallas kernels, fused(): pl.pallas_call(update_kernel, grid=(half // blk,), out_shape=jax.ShapeDty...  2.9 us

profile of v1, /device:TPU:0, one launch (start us, length us, event | category | flops | bytes accessed | tf_op | source)
XLA Modules:
  0.0 63.6 jit_solution(2762988783384518113)
XLA Ops:
  0.6 0.8 %copy.12.ids_ref = s32[128,1]{1,0:T(8,128)S(1)} copy(s32[128,1]{0,1:T(1,128)} %bitcast.11) | data formatting | bytes 1024 | tf_op jit(solution)/shard_map/squeeze | solution.py:337
  1.4 1.3 %copy.10 = bf16[1,128,2080]{2,1,0:T(8,128)(2,1)S(1)} copy(bf16[1,128,2080]{1,2,0:T(8,128)(2,1)} %param.6) | data formatting | bytes 1064960 | tf_op args[0]
  2.7 0.0 copy-start.2
  2.7 0.0 copy-start.3
  2.8 0.0 copy-start.4
  2.8 9.3 %copy.11 = bf16[1,1536,2080]{2,1,0:T(8,128)(2,1)} copy(bf16[1,1536,2080]{1,2,0:T(8,128)(2,1)} %param.9) | data formatting | bytes 12779520 | tf_op args[3]
  12.0 0.0 copy-done.2
  12.0 0.0 copy-done.3
  12.0 0.0 copy-done.4
  12.1 0.0 copy-start
  12.1 2.9 %copy-done = bf16[1,1536,2080]{2,1,0:T(8,128)(2,1)S(1)} copy-done((bf16[1,1536,2080]{2,1,0:T(8,128)(2,1)S(1)}, bf16[1,1536,2080]{2,1,0:T(8,128)(2,1)}, u32[]{:S(2)}) %copy-start) | copy-done | bytes 6389784
  15.0 33.6 %shard_map.93 = (bf16[192,1536]{1,0:T(8,128)(2,1)S(1)}, f32[1,768]{1,0:T(1,128)S(1)}, f32[1,2080]{1,0:T(1,128)S(1)}, f32[1,2080]{1,0:T(1,128)S(1)}, f32[768,1]{1...) custom-call(bf16[128,2080]{1,0:T(8,128)(2,1)S(1)} %bitcast.8, s32[128,1]{1,0:T(8,128)S(1)} %copy.12.ids_ref, ...), custom_call_target="tpu_custom_call" | custom-call | tf_op jit(solution)/shard_map/pallas_call | solution.py:307
  48.6 2.9 %shard_map.94 = f32[768,2080]{1,0:T(8,128)S(1)} custom-call(bf16[768,384]{1,0:T(8,128)(2,1)S(1)} %get-tuple-element.12.ht_ref, bf16[384,2176]{1,0:T(8,128)(2,1)S(1)} %get-tuple-element.13.rec_ref, f32[768,1]{1,0:T(8,128)S(1)} %get-tuple-element.14.rfac_ref, f32[1,2080]{1,0:T(1,128)S(1)} %get-tuple-element.15.cfac_ref), custom_call_target="tpu_custom_call" | custom-call | tf_op jit(solution)/shard_map/pallas_call | solution.py:339
  51.5 0.0 copy-start.1
  51.5 2.7 %copy-done.1 = f32[768,2080]{1,0:T(8,128)} copy-done((f32[768,2080]{1,0:T(8,128)}, f32[768,2080]{1,0:T(8,128)S(1)}, u32[]{:S(2)}) %copy-start.1) | copy-done | bytes 6389784
  54.3 7.3 %copy.13 = f32[1,768,2080]{1,2,0:T(8,128)} copy(f32[1,768,2080]{2,1,0:T(8,128)} %bitcast.7) | data formatting | bytes 12779520
  61.6 0.8 %copy.17 = bf16[1,1,192,1536]{3,2,1,0:T(8,128)(2,1)} copy(bf16[1,1,192,1536]{3,2,1,0:T(8,128)(2,1)S(1)} %bitcast.10) | data formatting | bytes 1179648
  62.4 0.6 copy.18
  63.0 0.6 copy.19
Async XLA Ops:
  2.7 9.3 %copy-start.2 = (bf16[1,1,192,1536]{3,2,1,0:T(8,128)(2,1)S(1)}, bf16[1,1,192,1536]{3,2,1,0:T(8,128)(2,1)}, u32[]{:S(2)}) copy-start(bf16[1,1,192,1536]{3,2,1,0:T(8,128)(2,1)} %param.8) | copy-start | bytes 1769476
  2.7 9.3 %copy-start.3 = (f32[1,2080]{1,0:T(1,128)S(1)}, f32[1,2080]{1,0:T(1,128)}, u32[]{:S(2)}) copy-start(f32[1,2080]{1,0:T(1,128)} %col_ref.1) | copy-start | bytes 24964
  2.8 9.3 %copy-start.4 = (f32[1,768]{1,0:T(1,128)S(1)}, f32[1,768]{1,0:T(1,128)}, u32[]{:S(2)}) copy-start(f32[1,768]{1,0:T(1,128)} %row_ref.1) | copy-start | bytes 9220
  12.1 2.9 %copy-start = (bf16[1,1536,2080]{2,1,0:T(8,128)(2,1)S(1)}, bf16[1,1536,2080]{2,1,0:T(8,128)(2,1)}, u32[]{:S(2)}) copy-start(bf16[1,1536,2080]{2,1,0:T(8,128)(2,1)} %copy.11) | copy-start | bytes 19169284
  51.5 2.8 %copy-start.1 = (f32[768,2080]{1,0:T(8,128)}, f32[768,2080]{1,0:T(8,128)S(1)}, u32[]{:S(2)}) copy-start(f32[768,2080]{1,0:T(8,128)S(1)} %shard_map.94) | copy-start | bytes 19169284

commit v2 on v1

--- a/solution.py
+++ b/solution.py
@@ -78,13 +78,13 @@
 
 def exchange_kernel(
     n, cap, tok_ref, ids_ref, hid_ref, w_hbm, row_ref, col_ref,
-    hg_ref, rownew_ref, colnew_ref, cfac_ref, rfac_ref, ht_hbm, rec_hbm,
-    outb, zb, parts, hs, ht, w, st, rowcol, w_sem, loc_sem, send_sem, recv_sem,
+    hg_ref, rownew_ref, colnew_ref, cfac_ref, rfac_ref, hs_hbm, rec_hbm,
+    outb, zb, parts, hs, w, st, rowcol, colst, w_sem, loc_sem, send_sem, recv_sem,
 ):
     e = lax.axis_index("expert")
     m = lax.axis_index("mp")
     r = lax.axis_index("replica")
-    width = tok_ref.shape[1]
+    width = tok_ref.shape[0]
     slots = n * cap
     half = hs.shape[1]
     rem = width - 4 * CH
@@ -108,20 +108,23 @@
     for k in range(1, n):
         pl.semaphore_signal(barrier, inc=1, device_id=along(k), device_id_type=MESH)
 
-    tc = tok_ref.shape[0]
-    ids = jnp.broadcast_to(ids_ref[...].astype(f32), (tc, tc))
-    ids_t = ids.T
+    tc = tok_ref.shape[1]
+    nt = (((1,), (1,)), ((), ()))
+    ids_t = jnp.broadcast_to(ids_ref[...].astype(f32), (tc, tc))
+    ids = ids_t.T
     p_i = lax.broadcasted_iota(jnp.int32, (tc, tc), 0)
     q_i = lax.broadcasted_iota(jnp.int32, (tc, tc), 1)
     before = jnp.where((p_i < q_i) & (ids == ids_t), 1.0, 0.0)
     slot = ids_t[0:1, :] * cap + jnp.sum(before, axis=0, keepdims=True)
     want = lax.broadcasted_iota(jnp.int32, (slots, tc), 0).astype(f32)
     dispatch = jnp.where(want == slot, 1.0, 0.0).astype(jnp.bfloat16)
-    mine = tok_ref[:, pl.ds(pl.multiple_of(m * CH, CH), CH)]
-    outb[:, 0:CH] = jnp.dot(dispatch, mine, preferred_element_type=f32).astype(jnp.bfloat16)
+    mine = tok_ref[pl.ds(pl.multiple_of(m * CH, CH), CH), :]
+    outb[:, 0:CH] = lax.dot_general(
+        dispatch, mine, nt, preferred_element_type=f32
+    ).astype(jnp.bfloat16)
     outb[:, CH:] = jnp.zeros((slots, REM), jnp.bfloat16)
-    outb[:, CH:CH + rem] = jnp.dot(
-        dispatch, tok_ref[:, 4 * CH:], preferred_element_type=f32
+    outb[:, CH:CH + rem] = lax.dot_general(
+        dispatch, tok_ref[4 * CH:, :], nt, preferred_element_type=f32
     ).astype(jnp.bfloat16)
     pl.semaphore_wait(barrier, 7 + n - 1)
 
@@ -156,6 +159,7 @@
         xc.append(send(zb.at[a, :], zb.at[b, :], across(4)))
         yo.append(send(zb.at[a, 0:CH], parts.at[m, a, :], across(2)))
         co.append(send(zb.at[a, 0:CH], parts.at[m, a, :], across(1)))
+    for k in range(n):
         piece = pl.ds(k * cap, cap)
         there = pl.ds(slots + k * cap, cap)
         hc.append(send(hid_ref.at[piece, other_half], hs.at[there, :], across(4)))
@@ -177,16 +181,14 @@
         fo[k].wait_recv()
     w_copy.wait()
 
-    nt = (((1,), (1,)), ((), ()))
-
     def hidden_tile(t):
         f = pl.ds(pl.multiple_of(t * 256, 256), 256)
-        acc = lax.dot_general(
-            zb[0:slots, CH:CH + rem], w[f, 4 * CH:], nt, preferred_element_type=f32
+        acc = jnp.dot(
+            zb[0:slots, CH:CH + rem], w[4 * CH:, f], preferred_element_type=f32
         )
         for c in range(4):
-            acc += lax.dot_general(
-                parts[c, 0:slots, :], w[f, c * CH:(c + 1) * CH], nt, preferred_element_type=f32
+            acc += jnp.dot(
+                parts[c, 0:slots, :], w[c * CH:(c + 1) * CH, f], preferred_element_type=f32
             )
         hg_ref[:, f] = acc.astype(jnp.bfloat16)
 
@@ -214,6 +216,7 @@
             parts.at[c], rec_hbm.at[:, pl.ds(c * CH, CH)], loc_sem.at[c]))
     local.append(pltpu.make_async_copy(
         zb.at[:, pl.ds(CH, REM)], rec_hbm.at[:, pl.ds(4 * CH, REM)], loc_sem.at[4]))
+    local.append(pltpu.make_async_copy(hs, hs_hbm, loc_sem.at[5]))
     for c in local:
         c.start()
 
@@ -224,7 +227,6 @@
         total, cols, weights = carry
         i = pl.ds(pl.multiple_of(t * blk, blk), blk)
         h = hs[:, i].T
-        ht[i, :] = h
         gg = []
         for c in range(5):
             rhs = parts[c] if c < 4 else zb[:, CH:CH + REM]
@@ -233,7 +235,6 @@
         rs = sum(jnp.sum(x, axis=1, keepdims=True) for x in gg)
         mean = rs / width + tiny_square
         new = decay_rate * rowcol[i, 0:1] + (1.0 - decay_rate) * mean
-        rfac_ref[i, :] = lax.rsqrt(new)
         rowcol[i, :] = jnp.broadcast_to(new, (blk, 128))
         inv = 1.0 / new
         total = total + jnp.sum(new, axis=0, keepdims=True)
@@ -251,45 +252,47 @@
     for j in range(17):
         c, o = j // 4, (j % 4) * 128
         st[me, j:j + 1, :] = cols[c][:, o:o + 128]
-        st[me, 17 + j:18 + j, :] = weights[c][:, o:o + 128]
-    st[me, 34:35, :] = jnp.broadcast_to(total, (1, 128))
-    st[me, 35:40, :] = jnp.zeros((5, 128), f32)
+        st[me, 24 + j:25 + j, :] = weights[c][:, o:o + 128]
+    st[me, 17:24, :] = jnp.zeros((7, 128), f32)
+    st[me, 41:48, :] = jnp.broadcast_to(total, (7, 128))
     sc = [send(st.at[me], st.at[me], across(d)) for d in range(1, 8)]
-    ht_copy = pltpu.make_async_copy(ht, ht_hbm, loc_sem.at[5])
-    ht_copy.start()
-    rownew_ref[...] = rowcol[...].T[0:1, :]
+    row_new = rowcol[...].T[0:1, :]
+    rownew_ref[...] = row_new
+    rfac_ref[...] = lax.rsqrt(row_new)
+    colst[...] = jnp.ones((24, 128), f32)
+    for j in range(17):
+        hi = min(width, (j + 1) * 128)
+        colst[j:j + 1, 0:hi - j * 128] = col_ref[:, j * 128:hi]
     for c in sc:
         c.wait_recv()
     tot = st[0]
     for j in range(1, 8):
         tot = tot + st[j]
 
-    def flat(base):
-        x = jnp.concatenate([tot[base + j:base + j + 1, :] for j in range(17)], axis=1)
-        return x[:, 0:width]
-
-    col_new = decay_rate * col_ref[...] + (1.0 - decay_rate) * (flat(0) / FF)
-    row_mean = tot[34:35, 0:1] / FF
-    colnew_ref[...] = col_new
-    ratio = jnp.sum(flat(17) / col_new, axis=1, keepdims=True)
+    col_new = decay_rate * colst[...] + (1.0 - decay_rate) * (tot[0:24] / FF)
+    row_mean = tot[47:48, 0:1] / FF
+    weighted = jnp.where(lax.broadcasted_iota(jnp.int32, (24, 128), 0) < 17, tot[24:48], 0.0)
+    ratio = jnp.sum(weighted / col_new, axis=0, keepdims=True)
+    ratio = jnp.sum(ratio, axis=1, keepdims=True)
     rms = jnp.sqrt(row_mean * ratio / (FF * width))
     scale = jnp.sqrt(row_mean) / jnp.maximum(1.0, rms / clip_limit)
-    cfac_ref[...] = lax.rsqrt(col_new) * scale
+    cfac = lax.rsqrt(col_new) * scale
+    cfac = jnp.concatenate([cfac, jnp.zeros((104, 128), f32)], axis=0).T
+    for j in range(17):
+        hi = min(width, (j + 1) * 128)
+        colnew_ref[:, j * 128:hi] = col_new[j:j + 1, 0:hi - j * 128]
+        cfac_ref[j * 128:hi, :] = cfac[0:hi - j * 128, j:j + 1]
     for c in started:
         c.wait_send()
     for c in local:
         c.wait()
-    ht_copy.wait()
-
-
-def update_kernel(ht_ref, rec_ref, rfac_ref, cfac_ref, out_ref):
-    width = out_ref.shape[1]
-    h = ht_ref[...]
-    rf = rfac_ref[...]
-    for c in range(5):
-        lo, hi = c * CH, min(width, (c + 1) * CH)
-        g = jnp.dot(h, rec_ref[:, lo:hi], preferred_element_type=jnp.float32)
-        out_ref[:, lo:hi] = (g * rf) * cfac_ref[:, lo:hi]
+
+
+def update_kernel(hs_ref, rec_ref, rfac_ref, cfac_ref, out_ref):
+    g = lax.dot_general(
+        rec_ref[...], hs_ref[...], (((0,), (0,)), ((), ())), preferred_element_type=jnp.float32
+    )
+    out_ref[...] = ((g * rfac_ref[...]) * cfac_ref[...])[0:out_ref.shape[0], :]
 
 
 def fused(grad_out, route, hidden_act, out_weight, row_state, col_state):
@@ -304,15 +307,15 @@
     hbm = pl.BlockSpec(memory_space=pl.ANY)
     wide = 4 * CH + REM
     copies = 9 * n + n - 1 + 7
-    hg, row_new, col_new, cfac, rfac, ht, rec = pl.pallas_call(
+    hg, row_new, col_new, cfac, rfac, hs, rec = pl.pallas_call(
         functools.partial(exchange_kernel, n, cap),
         out_shape=[
             jax.ShapeDtypeStruct((slots, ff), bf16),
             jax.ShapeDtypeStruct((1, half), f32),
             jax.ShapeDtypeStruct((1, width), f32),
-            jax.ShapeDtypeStruct((1, width), f32),
-            jax.ShapeDtypeStruct((half, 1), f32),
-            jax.ShapeDtypeStruct((half, 2 * slots), bf16),
+            jax.ShapeDtypeStruct((width, 1), f32),
+            jax.ShapeDtypeStruct((1, half), f32),
+            jax.ShapeDtypeStruct((2 * slots, half), bf16),
             jax.ShapeDtypeStruct((2 * slots, wide), bf16),
         ],
         in_specs=[vmem, vmem, vmem, hbm, vmem, vmem],
@@ -322,33 +325,35 @@
             pltpu.VMEM((2 * slots, CH + REM), bf16),
             pltpu.VMEM((4, 2 * slots, CH), bf16),
             pltpu.VMEM((2 * slots, half), bf16),
-            pltpu.VMEM((half, 2 * slots), bf16),
-            pltpu.VMEM((ff, width), bf16),
-            pltpu.VMEM((8, 40, 128), f32),
+            pltpu.VMEM((width, ff), bf16),
+            pltpu.VMEM((8, 48, 128), f32),
             pltpu.VMEM((half, 128), f32),
+            pltpu.VMEM((24, 128), f32),
             pltpu.SemaphoreType.DMA,
             pltpu.SemaphoreType.DMA((6,)),
             pltpu.SemaphoreType.DMA((copies,)),
             pltpu.SemaphoreType.DMA((copies,)),
         ],
         compiler_params=pltpu.CompilerParams(
-            collective_id=0, has_side_effects=True, vmem_limit_bytes=40 * 1024 * 1024
+            collective_id=0, has_side_effects=True, vmem_limit_bytes=58 * 1024 * 1024
         ),
-    )(grad_out[0], route[0], hidden_act[0, 0], out_weight[0], row_state, col_state)
-    blk = 128
+    )(
+        grad_out[0].T, route[0].T, hidden_act[0, 0], out_weight[0].T, row_state, col_state
+    )
+    blk = 256
     update = pl.pallas_call(
         update_kernel,
-        grid=(half // blk,),
-        out_shape=jax.ShapeDtypeStruct((half, width), f32),
+        grid=(pl.cdiv(width, blk),),
+        out_shape=jax.ShapeDtypeStruct((width, half), f32),
         in_specs=[
-            pl.BlockSpec((blk, 2 * slots), lambda i: (i, 0)),
-            pl.BlockSpec((2 * slots, wide), lambda i: (0, 0)),
+            pl.BlockSpec((2 * slots, half), lambda i: (0, 0)),
+            pl.BlockSpec((2 * slots, blk), lambda i: (0, i)),
+            pl.BlockSpec((1, half), lambda i: (0, 0)),
             pl.BlockSpec((blk, 1), lambda i: (i, 0)),
-            pl.BlockSpec((1, width), lambda i: (0, 0)),
         ],
-        out_specs=pl.BlockSpec((blk, width), lambda i: (i, 0)),
-        compiler_params=pltpu.CompilerParams(vmem_limit_bytes=32 * 1024 * 1024),
-    )(ht, rec, rfac, cfac)
+        out_specs=pl.BlockSpec((blk, half), lambda i: (i, 0)),
+        compiler_params=pltpu.CompilerParams(vmem_limit_bytes=58 * 1024 * 1024),
+    )(hs, rec, rfac, cfac).T
     return hg[None, None], update[None], row_new, col_new
 
 

time: 64.1 us -> 47.1 us (0.73)
  local copies, waits for them, and re-layouts: 26.3 us -> 2 us
  Pallas kernels: 36.6 us -> 44.1 us
    unnamed x16 -> x9, local copies, waits for them, and re-layouts: 25.6 us -> 2 us
    pallas_call x1, Pallas kernels: 2.9 us -> 9.05 us  [fused(): pl.pallas_call(update_kernel, grid=(pl.cdiv(width, blk),), out_shape=jax....]
    pallas_call x1, Pallas kernels: 33.6 us -> 35 us  [fused(): pl.pallas_call(functools.partial(exchange_kernel, n, cap), out_shape=[jax...]
    squeeze x1 -> x0, local copies, waits for them, and re-layouts: 0.76 us -> none  [fused(): route[0]]
where the time goes in v2:
time: 47.1 us; the launch traced here: 46.7 us
  Pallas kernels  44.1 us (94%)
  local copies, waits for them, and re-layouts  2 us (4%)
  between operations  0.67 us (1%)
    pallas_call x1, Pallas kernels, fused(): pl.pallas_call(functools.partial(exchange_kernel, n, cap), out_shape=[jax...  35 us
    pallas_call x1, Pallas kernels, fused(): pl.pallas_call(update_kernel, grid=(pl.cdiv(width, blk),), out_shape=jax....  9.05 us
    unnamed x9, local copies, waits for them, and re-layouts  2 us

profile of v2, /device:TPU:0, one launch (start us, length us, event | category | flops | bytes accessed | tf_op | source)
XLA Modules:
  0.0 46.7 jit_solution(874689371102358331)
XLA Ops:
  0.6 35.0 %shard_map.93 = (bf16[192,1536]{1,0:T(8,128)(2,1)}, f32[1,768]{1,0:T(1,128)}, f32[1,2080]{1,0:T(1,128)}, f32[2080,1]{1,0:T(8,128)}, f32[1,768]{1,0:T(1,128)}, /*...) custom-call(bf16[2080,128]{1,0:T(8,128)(2,1)} %bitcast.16, s32[1,128]{1,0:T(1,128)} %bitcast.17, ...), custom_call_target="tpu_custom_call" | custom-call | tf_op jit(solution)/shard_map/pallas_call | solution.py:310
  35.6 0.0 copy-start
  35.7 0.0 copy-start.2
  35.7 0.0 copy-start.1
  35.7 9.0 %shard_map.94 = f32[2080,768]{1,0:T(8,128)} custom-call(bf16[384,768]{1,0:T(8,128)(2,1)} %get-tuple-element.12.hs_ref, bf16[384,2176]{1,0:T(8,128)(2,1)} %get-tuple-element.13.rec_ref, f32[1,768]{1,0:T(1,128)} %get-tuple-element.14.rfac_ref, f32[2080,1]{1,0:T(8,128)} %get-tuple-element.15.cfac_ref), custom_call_target="tpu_custom_call" | custom-call | tf_op jit(solution)/shard_map/pallas_call | solution.py:344
  44.7 0.0 copy-done
  44.7 0.8 %copy.13 = bf16[1,1,192,1536]{3,2,1,0:T(8,128)(2,1)} copy(bf16[1,1,192,1536]{3,2,1,0:T(8,128)(2,1)S(1)} %bitcast.15) | data formatting | bytes 1179648
  45.5 0.0 copy-done.2
  45.5 0.6 %copy.14 = f32[1,768]{1,0:T(1,128)} copy(f32[1,768]{1,0:T(1,128)S(1)} %copy-done.2) | data formatting | bytes 6144
  46.1 0.0 copy-done.1
  46.1 0.6 %copy.15 = f32[1,2080]{1,0:T(1,128)} copy(f32[1,2080]{1,0:T(1,128)S(1)} %copy-done.1) | data formatting | bytes 16640
Async XLA Ops:
  35.6 9.1 %copy-start = (bf16[192,1536]{1,0:T(8,128)(2,1)S(1)}, bf16[192,1536]{1,0:T(8,128)(2,1)}, u32[]{:S(2)}) copy-start(bf16[192,1536]{1,0:T(8,128)(2,1)} %get-tuple-element.11) | copy-start | bytes 1769476
  35.7 9.9 %copy-start.2 = (f32[1,768]{1,0:T(1,128)S(1)}, f32[1,768]{1,0:T(1,128)}, u32[]{:S(2)}) copy-start(f32[1,768]{1,0:T(1,128)} %get-tuple-element.24) | copy-start | bytes 9220
  35.7 10.5 %copy-start.1 = (f32[1,2080]{1,0:T(1,128)S(1)}, f32[1,2080]{1,0:T(1,128)}, u32[]{:S(2)}) copy-start(f32[1,2080]{1,0:T(1,128)} %get-tuple-element.25) | copy-start | bytes 24964

commit v3 on v2

--- a/solution.py
+++ b/solution.py
@@ -232,23 +232,25 @@
             rhs = parts[c] if c < 4 else zb[:, CH:CH + REM]
             g = jnp.dot(h, rhs, preferred_element_type=f32)
             gg.append(g * g)
-        rs = sum(jnp.sum(x, axis=1, keepdims=True) for x in gg)
+        lanes = sum(x[:, o:o + 128] for x in gg for o in range(0, x.shape[1], 128))
+        rs = jnp.sum(lanes, axis=1, keepdims=True)
         mean = rs / width + tiny_square
         new = decay_rate * rowcol[i, 0:1] + (1.0 - decay_rate) * mean
         rowcol[i, :] = jnp.broadcast_to(new, (blk, 128))
         inv = 1.0 / new
         total = total + jnp.sum(new, axis=0, keepdims=True)
         cols = tuple(
-            a + jnp.sum(x, axis=0, keepdims=True) for a, x in zip(cols, gg))
+            a + jnp.sum(x.reshape(blk // 8, 8, -1), axis=0) for a, x in zip(cols, gg))
         weights = tuple(
-            a + jnp.sum(x * inv, axis=0, keepdims=True) for a, x in zip(weights, gg))
+            a + jnp.sum((x * inv).reshape(blk // 8, 8, -1), axis=0) for a, x in zip(weights, gg))
         return total, cols, weights
 
-    zero = tuple(jnp.zeros((1, CH if c < 4 else REM), f32) for c in range(5))
+    zero = tuple(jnp.zeros((8, CH if c < 4 else REM), f32) for c in range(5))
     total, cols, weights = lax.fori_loop(
         0, half // blk, block, (jnp.zeros((1, 1), f32), zero, zero))
     me = m * 2 + r
-    cols = [x + half * tiny_square for x in cols]
+    cols = [jnp.sum(x, axis=0, keepdims=True) + half * tiny_square for x in cols]
+    weights = [jnp.sum(x, axis=0, keepdims=True) for x in weights]
     for j in range(17):
         c, o = j // 4, (j % 4) * 128
         st[me, j:j + 1, :] = cols[c][:, o:o + 128]
@@ -288,7 +290,13 @@
         c.wait()
 
 
-def update_kernel(hs_ref, rec_ref, rfac_ref, cfac_ref, out_ref):
+def update_kernel(
+    hs_ref, rec_ref, rfac_ref, cfac_ref, hg_ref, row_ref, col_ref,
+    out_ref, hg_out, row_out, col_out,
+):
+    hg_out[...] = hg_ref[...]
+    row_out[...] = row_ref[...]
+    col_out[...] = col_ref[...]
     g = lax.dot_general(
         rec_ref[...], hs_ref[...], (((0,), (0,)), ((), ())), preferred_element_type=jnp.float32
     )
@@ -340,21 +348,35 @@
     )(
         grad_out[0].T, route[0].T, hidden_act[0, 0], out_weight[0].T, row_state, col_state
     )
-    blk = 256
-    update = pl.pallas_call(
+    blk = 1024
+    steps = pl.cdiv(width, blk)
+    update, hg, row_new, col_new = pl.pallas_call(
         update_kernel,
-        grid=(pl.cdiv(width, blk),),
-        out_shape=jax.ShapeDtypeStruct((width, half), f32),
+        grid=(steps,),
+        out_shape=[
+            jax.ShapeDtypeStruct((width, half), f32),
+            jax.ShapeDtypeStruct((slots, ff), bf16),
+            jax.ShapeDtypeStruct((1, half), f32),
+            jax.ShapeDtypeStruct((1, width), f32),
+        ],
         in_specs=[
             pl.BlockSpec((2 * slots, half), lambda i: (0, 0)),
             pl.BlockSpec((2 * slots, blk), lambda i: (0, i)),
             pl.BlockSpec((1, half), lambda i: (0, 0)),
             pl.BlockSpec((blk, 1), lambda i: (i, 0)),
+            pl.BlockSpec((slots // steps, ff), lambda i: (i, 0)),
+            pl.BlockSpec((1, half), lambda i: (0, 0)),
+            pl.BlockSpec((1, width), lambda i: (0, 0)),
         ],
-        out_specs=pl.BlockSpec((blk, half), lambda i: (i, 0)),
+        out_specs=[
+            pl.BlockSpec((blk, half), lambda i: (i, 0)),
+            pl.BlockSpec((slots // steps, ff), lambda i: (i, 0)),
+            pl.BlockSpec((1, half), lambda i: (0, 0)),
+            pl.BlockSpec((1, width), lambda i: (0, 0)),
+        ],
         compiler_params=pltpu.CompilerParams(vmem_limit_bytes=58 * 1024 * 1024),
-    )(hs, rec, rfac, cfac).T
-    return hg[None, None], update[None], row_new, col_new
+    )(hs, rec, rfac, cfac, hg, row_new, col_new)
+    return hg[None, None], update.T[None], row_new, col_new
 
 
 def solution(mesh):

time: 47.1 us -> 41.8 us (0.89)
  Pallas kernels: 44.1 us -> 41 us
  local copies, waits for them, and re-layouts: 2 us -> 0 us
    pallas_call x1, Pallas kernels: 9.05 us -> 6.08 us  [fused(): pl.pallas_call(update_kernel, grid=(steps,), out_shape=[jax.ShapeDtypeStr...]
    unnamed x9 -> x0, local copies, waits for them, and re-layouts: 2 us -> none
where the time goes in v3:
time: 41.8 us; the launch traced here: 41.6 us
  Pallas kernels  41 us (98%)
  between operations  0.64 us (2%)
    pallas_call x1, Pallas kernels, fused(): pl.pallas_call(functools.partial(exchange_kernel, n, cap), out_shape=[jax...  34.9 us
    pallas_call x1, Pallas kernels, fused(): pl.pallas_call(update_kernel, grid=(steps,), out_shape=[jax.ShapeDtypeStr...  6.08 us

profile of v3, /device:TPU:0, one launch (start us, length us, event | category | flops | bytes accessed | tf_op | source)
XLA Modules:
  0.0 41.6 jit_solution(6580567202644487296)
XLA Ops:
  0.6 34.9 %shard_map.93 = (bf16[192,1536]{1,0:T(8,128)(2,1)}, f32[1,768]{1,0:T(1,128)}, f32[1,2080]{1,0:T(1,128)}, f32[2080,1]{1,0:T(8,128)}, f32[1,768]{1,0:T(1,128)}, /*...) custom-call(bf16[2080,128]{1,0:T(8,128)(2,1)} %bitcast.14, s32[1,128]{1,0:T(1,128)} %bitcast.15, ...), custom_call_target="tpu_custom_call" | custom-call | tf_op jit(solution)/shard_map/pallas_call | solution.py:318
  35.5 6.1 %shard_map.94 = (f32[2080,768]{1,0:T(8,128)}, bf16[192,1536]{1,0:T(8,128)(2,1)}, f32[1,768]{1,0:T(1,128)}, f32[1,2080]{1,0:T(1,128)}) custom-call(bf16[384,768]{1,0:T(8,128)(2,1)} %get-tuple-element.15.hs_ref, bf16[384,2176]{1,0:T(8,128)(2,1)} %get-tuple-element.16.rec_ref, f32[1,768]{1,0:T(1,128)} %get-tuple-element.17.rfac_ref, ...), custom_call_target="tpu_custom_call" | custom-call | tf_op jit(solution)/shard_map/pallas_call | solution.py:353

commit v4 on v3

--- a/solution.py
+++ b/solution.py
@@ -77,9 +77,9 @@
 
 
 def exchange_kernel(
-    n, cap, tok_ref, ids_ref, hid_ref, w_hbm, row_ref, col_ref,
-    hg_ref, rownew_ref, colnew_ref, cfac_ref, rfac_ref, hs_hbm, rec_hbm,
-    outb, zb, parts, hs, w, st, rowcol, colst, w_sem, loc_sem, send_sem, recv_sem,
+    n, cap, tok_hbm, ids_ref, hid_hbm, w_hbm, row_ref, col_ref,
+    hg_hbm, rownew_ref, colnew_ref, cfac_ref, rfac_ref, hs_hbm, rec_hbm,
+    outb, zb, parts, hs, w, st, rowcol, colst, tok_ref, hid_ref, hg_ref, w_sem, loc_sem, send_sem, recv_sem,
 ):
     e = lax.axis_index("expert")
     m = lax.axis_index("mp")
@@ -90,8 +90,11 @@
     rem = width - 4 * CH
     f32 = jnp.float32
 
+    tok_copy = pltpu.make_async_copy(tok_hbm, tok_ref, loc_sem.at[6])
+    tok_copy.start()
+    hid_copy = pltpu.make_async_copy(hid_hbm, hid_ref, loc_sem.at[7])
+    hid_copy.start()
     w_copy = pltpu.make_async_copy(w_hbm, w, w_sem)
-    w_copy.start()
 
     def across(d):
         m2 = m + (1 - 2 * (m % 2)) * (d % 2)
@@ -118,6 +121,8 @@
     slot = ids_t[0:1, :] * cap + jnp.sum(before, axis=0, keepdims=True)
     want = lax.broadcasted_iota(jnp.int32, (slots, tc), 0).astype(f32)
     dispatch = jnp.where(want == slot, 1.0, 0.0).astype(jnp.bfloat16)
+    tok_copy.wait()
+    w_copy.start()
     mine = tok_ref[pl.ds(pl.multiple_of(m * CH, CH), CH), :]
     outb[:, 0:CH] = lax.dot_general(
         dispatch, mine, nt, preferred_element_type=f32
@@ -159,6 +164,7 @@
         xc.append(send(zb.at[a, :], zb.at[b, :], across(4)))
         yo.append(send(zb.at[a, 0:CH], parts.at[m, a, :], across(2)))
         co.append(send(zb.at[a, 0:CH], parts.at[m, a, :], across(1)))
+    hid_copy.wait()
     for k in range(n):
         piece = pl.ds(k * cap, cap)
         there = pl.ds(slots + k * cap, cap)
@@ -204,6 +210,8 @@
         yx[k].wait_recv()
         b = rows_of(k, slots)
         fx.append(send(parts.at[m_y, b, :], parts.at[m_y, b, :], across(1)))
+    hg_copy = pltpu.make_async_copy(hg_ref, hg_hbm, loc_sem.at[8])
+    hg_copy.start()
     parts[m, slots:, :] = zb[slots:, 0:CH]
     for k in range(n):
         hc[k].wait_recv()
@@ -288,6 +296,7 @@
         c.wait_send()
     for c in local:
         c.wait()
+    hg_copy.wait()
 
 
 def update_kernel(
@@ -326,8 +335,8 @@
             jax.ShapeDtypeStruct((2 * slots, half), bf16),
             jax.ShapeDtypeStruct((2 * slots, wide), bf16),
         ],
-        in_specs=[vmem, vmem, vmem, hbm, vmem, vmem],
-        out_specs=[vmem] * 5 + [hbm] * 2,
+        in_specs=[hbm, vmem, hbm, hbm, vmem, vmem],
+        out_specs=[hbm] + [vmem] * 4 + [hbm] * 2,
         scratch_shapes=[
             pltpu.VMEM((slots, CH + REM), bf16),
             pltpu.VMEM((2 * slots, CH + REM), bf16),
@@ -337,8 +346,11 @@
             pltpu.VMEM((8, 48, 128), f32),
             pltpu.VMEM((half, 128), f32),
             pltpu.VMEM((24, 128), f32),
+            pltpu.VMEM((width, tok_count), bf16),
+            pltpu.VMEM((slots, ff), bf16),
+            pltpu.VMEM((slots, ff), bf16),
             pltpu.SemaphoreType.DMA,
-            pltpu.SemaphoreType.DMA((6,)),
+            pltpu.SemaphoreType.DMA((9,)),
             pltpu.SemaphoreType.DMA((copies,)),
             pltpu.SemaphoreType.DMA((copies,)),
         ],

time: 41.8 us -> 41.2 us (0.986)
  Pallas kernels: 41 us -> 40.3 us
    pallas_call x1, Pallas kernels: 34.9 us -> 34.2 us  [fused(): pl.pallas_call(functools.partial(exchange_kernel, n, cap), out_shape=[jax...]
where the time goes in v4:
time: 41.2 us; the launch traced here: 41 us
  Pallas kernels  40.3 us (98%)
  between operations  0.64 us (2%)
    pallas_call x1, Pallas kernels, fused(): pl.pallas_call(functools.partial(exchange_kernel, n, cap), out_shape=[jax...  34.2 us
    pallas_call x1, Pallas kernels, fused(): pl.pallas_call(update_kernel, grid=(steps,), out_shape=[jax.ShapeDtypeStr...  6.07 us

profile of v4, /device:TPU:0, one launch (start us, length us, event | category | flops | bytes accessed | tf_op | source)
XLA Modules:
  0.0 41.0 jit_solution(5081509208755935553)
XLA Ops:
  0.6 34.2 %shard_map.93 = (bf16[192,1536]{1,0:T(8,128)(2,1)}, f32[1,768]{1,0:T(1,128)}, f32[1,2080]{1,0:T(1,128)}, f32[2080,1]{1,0:T(8,128)}, f32[1,768]{1,0:T(1,128)}, /*...) custom-call(bf16[2080,128]{1,0:T(8,128)(2,1)} %bitcast.14, s32[1,128]{1,0:T(1,128)} %bitcast.15, ...), custom_call_target="tpu_custom_call" | custom-call | tf_op jit(solution)/shard_map/pallas_call | solution.py:327
  34.9 6.1 %shard_map.94 = (f32[2080,768]{1,0:T(8,128)}, bf16[192,1536]{1,0:T(8,128)(2,1)}, f32[1,768]{1,0:T(1,128)}, f32[1,2080]{1,0:T(1,128)}) custom-call(bf16[384,768]{1,0:T(8,128)(2,1)} %get-tuple-element.15.hs_ref, bf16[384,2176]{1,0:T(8,128)(2,1)} %get-tuple-element.16.rec_ref, f32[1,768]{1,0:T(1,128)} %get-tuple-element.17.rfac_ref, ...), custom_call_target="tpu_custom_call" | custom-call | tf_op jit(solution)/shard_map/pallas_call | solution.py:365
